TPU v7x, 32 devices: a whole 2x2x4 slice. The times are simulated.
32 devices in a mesh: grp: 4 (over z), dev: 8 (over y, x, core).
Axes of the slice: x: 2, y: 2, z: 4, core: 2. Of those that a mesh axis runs over, the one named last changes fastest.
Arguments:
- pool: bfloat16 [98304, 1024], P(('grp', 'dev'))
- nearest: float32 [98304], P(('grp', 'dev')), may hold values from 0.5 to 2.2
- center_owner: int32 [4, 256], P('grp'), may hold values from 0 to 7, as said below
- center_offset: int32 [4, 256], P('grp'), may hold values from 0 to 3071
Outputs:
- nearest_after: float32 [98304], P(('grp', 'dev'))
Inputs may be any that keep to these rules, and one draw needn't show every extreme that they name: `center_owner`: in each group no more than 32 centers have the same owner, one owner has exactly 32, and the centers of a group are distinct rows.
All inputs are finite; a program needn't handle non-finite values.
Results may differ from a plain program's by a relative error of at most 0.0003.
Values may be sent and summed in bfloat16 or wider, within the bound.
A program may use at most 64 MiB of HBM per device.

v0:
```python
import math

import jax
import jax.numpy as jnp
from jax import lax
from jax.sharding import PartitionSpec as P

MOST = 32


def nearest_fold(pool_rows, row_norm, running, fragment):
    center_norm = jnp.einsum("cd,cd->c", fragment, fragment, preferred_element_type=jnp.float32)
    total_rows = pool_rows.shape[0]
    block = math.gcd(total_rows, 512)
    blocks = total_rows // block

    def one_block(args):
        block_rows, block_norm, block_near = args
        inner = lax.dot_general(
            block_rows, fragment, (((1,), (1,)), ((), ())), preferred_element_type=jnp.float32
        )
        distance = jnp.maximum(block_norm[:, None] + center_norm[None, :] - 2.0 * inner, 0.0)
        return jnp.minimum(block_near, jnp.min(distance, axis=1))

    result = lax.map(
        one_block,
        (
            pool_rows.reshape(blocks, block, pool_rows.shape[1]),
            row_norm.reshape(blocks, block),
            running.reshape(blocks, block),
        ),
    )
    return result.reshape(total_rows)


def shards(pool, nearest, center_owner, center_offset):
    owners = center_owner[0]
    offsets = center_offset[0]
    dev_count = lax.axis_size("dev")
    my_index = lax.axis_index("dev")
    per_device = owners.shape[0] // dev_count
    owner_hot = (owners[:, None] == jnp.arange(dev_count, dtype=jnp.int32)[None, :]).astype(
        jnp.int32
    )
    slot_rank = jnp.sum((jnp.cumsum(owner_hot, axis=0) - 1) * owner_hot, axis=1)
    chosen = (
        (owners == my_index)[None, :]
        & (slot_rank[None, :] == jnp.arange(MOST, dtype=jnp.int32)[:, None])
    ).astype(jnp.int32)
    slot_offsets = jnp.sum(chosen * offsets[None, :], axis=1)
    slot_rows = jnp.take(pool, slot_offsets, axis=0)
    every_slot = lax.all_gather(slot_rows, "dev", axis=0, tiled=True)
    slot_index = owners * MOST + slot_rank
    mine = lax.dynamic_slice_in_dim(slot_index, my_index * per_device, per_device)
    local_centers = jnp.take(every_slot, mine, axis=0)
    row_norm = jnp.einsum("rd,rd->r", pool, pool, preferred_element_type=jnp.float32)
    return nearest_fold(
        pool, row_norm, nearest, lax.all_gather(local_centers, ("grp", "dev"), axis=0, tiled=True)
    )


def solution(mesh):
    in_specs = (P(("grp", "dev"), None), P(("grp", "dev")), P("grp", None), P("grp", None))
    out_specs = P(("grp", "dev"))
    return jax.shard_map(shards, mesh=mesh, in_specs=in_specs, out_specs=out_specs, check_vma=False)
```

profile of v0, /device:TPU:0, one launch (start us, length us, event | category | flops | bytes accessed | tf_op | source)
XLA Modules:
  0.0 111.5 jit_solution(1585596497188410677)
XLA Ops:
  6.5 0.7 fusion.7
  7.2 0.6 reduce-window.6
  7.8 0.2 slice_reduce_fusion
  8.0 0.8 fusion.6
  8.8 0.7 multiply_add_fusion
  9.5 0.7 compare_reduce_fusion
  10.2 0.8 select_reduce_fusion
  11.0 0.1 compare_and_fusion.1
  11.1 4.3 %gather_fusion = bf16[32,1024]{1,0:T(8,128)(2,1)S(1)} fusion(bf16[3072,1024]{1,0:T(8,128)(2,1)} %param.6, s32[1024]{0:T(1024)S(1)} %pad_clamp_fusion.1), kind=kCustom, calls=%fused_computation | custom fusion | bytes 131200 | tf_op jit(solution)/shard_map/jit(_take)/gather | solution.py:51
  15.4 0.1 broadcast_select_fusion
  15.5 11.3 %all_gather.6 = bf16[256,1024]{1,0:T(8,128)(2,1)S(1)} all-gather(bf16[32,1024]{1,0:T(8,128)(2,1)S(1)} %broadcast_select_fusion), channel_id=1, replica_groups=mesh['grp'=4,'dev'=8] {'dev'}, dimensions={0}, use_global_device_ids=true | all-gather | bytes 589824 | tf_op jit(solution)/shard_map/all_gather | solution.py:52
  26.8 0.6 gather_fusion.1
  27.4 0.7 broadcast_select_fusion.1
  28.1 4.1 %fusion.3 = f32[3072]{0:T(1024)S(1)} fusion(bf16[3072,1024]{1,0:T(8,128)(2,1)} %param.6), kind=kLoop, calls=%fused_computation.9 | loop fusion | flops 9434112 | bytes 6303744 | tf_op jit(solution)/shard_map/rd,rd->r/dot_general | solution.py:56
  32.3 52.7 %all-gather.2.cloned.1.call-done = bf16[1024,1024]{1,0:T(8,128)(2,1)} async-done(((bf16[32,1024]{1,0:T(8,128)(2,1)}), bf16[1024,1024]{1,0:T(8,128)(2,1)}) %all-gather.2.cloned.1.call-update) | async-done | bytes 2097168 | tf_op jit(solution)/shard_map/all_gather | solution.py:58
  85.0 2.2 %fusion.4 = f32[1024]{0:T(1024)S(1)} fusion(bf16[1024,1024]{1,0:T(8,128)(2,1)} %all-gather.2.cloned.1.call-done), kind=kLoop, calls=%fused_computation.11 | loop fusion | flops 3144704 | bytes 2101248 | tf_op jit(solution)/shard_map/cd,cd->c/dot_general | solution.py:12
  87.2 16.8 %while.10 = (s32[]{:T(128)}, f32[6,512]{1,0:T(8,128)S(1)}, f32[6,512]{1,0:T(8,128)S(1)}, f32[6,512]{1,0:T(8,128)S(1)}, f32[1024]{0:T(1024)S(1)}, /*index=5*/bf16...) while((s32[]{:T(128)}, f32[6,512]{1,0:T(8,128)S(1)}, ...), condition=%wide.region_6.7_spmd, body=%wide.region_4.6_spmd.sunk | while | flops 1076363264 | bytes 3168873 | solution.py:25
  87.2 2.7 %maximum_reduce_fusion.2 = f32[512]{0:T(512)S(1)} fusion(bf16[1024,1024]{1,0:T(8,128)(2,1)S(1)} %get-tuple-element.126, bf16[6,512,1024]{2,1,0:T(8,128)(2,1)} %get-tuple-element.125, s32[]{:T(128)} %get-tuple-element.111, f32[1024]{0:T(1024)S(1)} %get-tuple-element.124, f32[512]{0:T(512)S(1)} %bitcast.30), kind=kOutput, calls=%fused_computation.2.clone.1 | convolution fusion | flops 1076362752 | bytes 3154432 | tf_op jit(solution)/shard_map/while/body/eval_jaxpr/dot_general | solution.py:19
  90.0 2.7 %maximum_reduce_fusion.2 = f32[512]{0:T(512)S(1)} fusion(bf16[1024,1024]{1,0:T(8,128)(2,1)S(1)} %get-tuple-element.126, bf16[6,512,1024]{2,1,0:T(8,128)(2,1)} %get-tuple-element.125, s32[]{:T(128)} %get-tuple-element.111, f32[1024]{0:T(1024)S(1)} %get-tuple-element.124, f32[512]{0:T(512)S(1)} %bitcast.30), kind=kOutput, calls=%fused_computation.2.clone.1 | convolution fusion | flops 1076362752 | bytes 3154432 | tf_op jit(solution)/shard_map/while/body/eval_jaxpr/dot_general | solution.py:19
  92.8 2.7 %maximum_reduce_fusion.2 = f32[512]{0:T(512)S(1)} fusion(bf16[1024,1024]{1,0:T(8,128)(2,1)S(1)} %get-tuple-element.126, bf16[6,512,1024]{2,1,0:T(8,128)(2,1)} %get-tuple-element.125, s32[]{:T(128)} %get-tuple-element.111, f32[1024]{0:T(1024)S(1)} %get-tuple-element.124, f32[512]{0:T(512)S(1)} %bitcast.30), kind=kOutput, calls=%fused_computation.2.clone.1 | convolution fusion | flops 1076362752 | bytes 3154432 | tf_op jit(solution)/shard_map/while/body/eval_jaxpr/dot_general | solution.py:19
  95.7 2.7 %maximum_reduce_fusion.2 = f32[512]{0:T(512)S(1)} fusion(bf16[1024,1024]{1,0:T(8,128)(2,1)S(1)} %get-tuple-element.126, bf16[6,512,1024]{2,1,0:T(8,128)(2,1)} %get-tuple-element.125, s32[]{:T(128)} %get-tuple-element.111, f32[1024]{0:T(1024)S(1)} %get-tuple-element.124, f32[512]{0:T(512)S(1)} %bitcast.30), kind=kOutput, calls=%fused_computation.2.clone.1 | convolution fusion | flops 1076362752 | bytes 3154432 | tf_op jit(solution)/shard_map/while/body/eval_jaxpr/dot_general | solution.py:19
  98.5 2.7 %maximum_reduce_fusion.2 = f32[512]{0:T(512)S(1)} fusion(bf16[1024,1024]{1,0:T(8,128)(2,1)S(1)} %get-tuple-element.126, bf16[6,512,1024]{2,1,0:T(8,128)(2,1)} %get-tuple-element.125, s32[]{:T(128)} %get-tuple-element.111, f32[1024]{0:T(1024)S(1)} %get-tuple-element.124, f32[512]{0:T(512)S(1)} %bitcast.30), kind=kOutput, calls=%fused_computation.2.clone.1 | convolution fusion | flops 1076362752 | bytes 3154432 | tf_op jit(solution)/shard_map/while/body/eval_jaxpr/dot_general | solution.py:19
  101.2 2.7 %maximum_reduce_fusion.2 = f32[512]{0:T(512)S(1)} fusion(bf16[1024,1024]{1,0:T(8,128)(2,1)S(1)} %get-tuple-element.126, bf16[6,512,1024]{2,1,0:T(8,128)(2,1)} %get-tuple-element.125, s32[]{:T(128)} %get-tuple-element.111, f32[1024]{0:T(1024)S(1)} %get-tuple-element.124, f32[512]{0:T(512)S(1)} %bitcast.30), kind=kOutput, calls=%fused_computation.2.clone.1 | convolution fusion | flops 1076362752 | bytes 3154432 | tf_op jit(solution)/shard_map/while/body/eval_jaxpr/dot_general | solution.py:19
  104.0 0.6 reshape.63
  (33 shorter events, 0.6 us)
Async XLA Ops:
  6.5 78.4 %all-gather.2.cloned.1.call-start = ((), (), s32[]{:S(2)}) async-start(), calls=%async_computation | async-start | bytes 2162688 | tf_op jit(solution)/shard_map/all_gather | solution.py:58
  28.1 4.1 %copy-start.1 = (f32[3072]{0:T(1024)S(1)}, f32[3072]{0:T(1024)}, u32[]{:S(2)}) copy-start(f32[3072]{0:T(1024)} %param.7) | copy-start | bytes 36868
  85.0 2.2 %copy-start = (bf16[1024,1024]{1,0:T(8,128)(2,1)S(1)}, bf16[1024,1024]{1,0:T(8,128)(2,1)}, u32[]{:S(2)}) copy-start(bf16[1024,1024]{1,0:T(8,128)(2,1)} %all-gather.2.cloned.1.call-done) | copy-start | bytes 6291460
Sparse Core Ops, SparseCore 0:
  28.2 56.6 all-gather.1
where the time goes:
time: 112 us; the launch traced here: 111 us
  waiting for transfers between devices  52.7 us (47%)
  matrix products  16.1 us (14%)
  between operations  13.5 us (12%)
  other arithmetic  11.5 us (10%)
  blocking collectives  11.3 us (10%)
  local copies, waits for them, and re-layouts  6.15 us (5%)
    all_gather x1, waiting for transfers between devices, shards(): lax.all_gather(local_centers, ('grp', 'dev'), axis=0, tiled=True)  52.7 us
    dot_general x6, matrix products, one_block(): lax.dot_general(block_rows, fragment, (((1,), (1,)), ((), ())), preferred...  16.1 us
    all_gather x1, blocking collectives, shards(): every_slot = lax.all_gather(slot_rows, 'dev', axis=0, tiled=True)  11.3 us
    gather x1, local copies, waits for them, and re-layouts, shards(): slot_rows = jnp.take(pool, slot_offsets, axis=0)  4.27 us
    dot_general x1, other arithmetic, shards(): jnp.einsum('rd,rd->r', pool, pool, preferred_element_type=jnp.float32)  4.09 us
  transfers between devices with their start and end apart: 1, of which 1 were waited for; matrix products, arithmetic and copies ran while one was open for 4% of the time, Pallas kernels for 0%

commit v1 on v0

v1 whole, which is shorter than its diff:
```python
import functools
import math

import jax
import jax.numpy as jnp
from jax import lax
from jax.experimental import pallas as pl
from jax.experimental.pallas import tpu as pltpu
from jax.sharding import PartitionSpec as P

MOST = 32
LANES = 128
MESH = pl.DeviceIdType.MESH
F32 = jnp.float32
NT = (((1,), (1,)), ((), ()))


def fused_kernel(
    owner_ref, offset_ref, nearest_ref, pool_hbm, out_ref,
    pool, union, picked, row_norm, half_norm, low,
    pool_sem, z_s, z_r, x_s, x_r, y_s, y_r, dx_s, dx_r, dy_s, dy_r, c_s, c_r,
):
    rows, width = pool.shape
    chunk = 256
    chunks = rows // chunk
    half = MOST // 2

    z = lax.axis_index("grp")
    dev = lax.axis_index("dev")
    core = dev % 2
    x = (dev // 2) % 2
    y = dev // 4
    chip = dev // 2
    x_dev = (y * 2 + (1 - x)) * 2 + core
    y_dev = ((1 - y) * 2 + x) * 2 + core
    c_dev = chip * 2 + (1 - core)
    x_chip = y * 2 + (1 - x)
    y_chip = (1 - y) * 2 + x
    d_chip = (1 - y) * 2 + (1 - x)
    layers = [z, z + 1 - 2 * (z % 2), (z + 2) % 4, 3 - z]

    barrier = pltpu.get_barrier_semaphore()
    peers = [(z, x_dev), (z, y_dev), (z, c_dev)] + [(l, dev) for l in layers[1:]]
    for peer in peers:
        pl.semaphore_signal(barrier, inc=1, device_id=peer, device_id_type=MESH)

    loads = [
        pltpu.make_async_copy(
            pool_hbm.at[pl.ds(c * chunk, chunk)], pool.at[pl.ds(c * chunk, chunk)], pool_sem.at[c]
        )
        for c in range(chunks)
    ]
    for load in loads:
        load.start()

    count = owner_ref.shape[1]
    hot = owner_ref[...] == dev
    hot_f = jnp.where(hot, 1.0, 0.0).astype(F32)
    before = lax.broadcasted_iota(jnp.int32, (count, count), 0) < lax.broadcasted_iota(
        jnp.int32, (count, count), 1
    )
    rank = jnp.dot(
        jnp.broadcast_to(hot_f, (8, count)).astype(jnp.bfloat16),
        jnp.where(before, 1.0, 0.0).astype(jnp.bfloat16),
        preferred_element_type=F32,
    )[0:1]
    slot = lax.broadcasted_iota(jnp.int32, (MOST, count), 0).astype(F32)
    chosen = jnp.where(slot == rank, 1.0, 0.0) * hot_f
    slot_offset = jnp.sum(chosen * offset_ref[...].astype(F32), axis=1, keepdims=True)

    column = lax.broadcasted_iota(jnp.int32, (MOST, chunk), 1).astype(F32)
    for c in range(chunks):
        loads[c].wait()
        one_hot = jnp.where(column + float(c * chunk) == slot_offset, 1.0, 0.0).astype(jnp.bfloat16)
        part = jnp.dot(one_hot, pool[pl.ds(c * chunk, chunk), :], preferred_element_type=F32)
        if c == 0:
            picked[...] = part
        else:
            picked[...] += part

    def place(layer, core_, chip_):
        return pl.multiple_of(((layer * 2 + core_) * 4 + chip_) * MOST, MOST)

    def copy(start, size, send, recv, to):
        ref = union.at[pl.ds(start, size)]
        return pltpu.make_async_remote_copy(
            src_ref=ref, dst_ref=ref, send_sem=send, recv_sem=recv, device_id=to, device_id_type=MESH
        )

    own = place(z, core, chip)
    union[pl.ds(own, MOST), :] = picked[...].astype(jnp.bfloat16)
    sent = []

    def send(*args):
        c = copy(*args)
        c.start()
        sent.append(c)

    def wait(start, size, send_sem, recv_sem, to):
        copy(start, size, send_sem, recv_sem, to).wait_recv()

    to_x, to_y, to_c = (z, x_dev), (z, y_dev), (z, c_dev)

    def spread(i):
        at = place(layers[i], core, chip)
        send(at, MOST, x_s.at[i], x_r.at[i], to_x)
        send(at, MOST, y_s.at[i], y_r.at[i], to_y)
        send(at, MOST, c_s.at[i], c_r.at[i], to_c)

    def along_z(k):
        send(own, MOST, z_s.at[k - 1], z_r.at[k - 1], (layers[k], dev))

    def from_z(k):
        wait(place(layers[k], core, chip), MOST, z_s.at[k - 1], z_r.at[k - 1], (layers[k], dev))
        spread(k)

    def relay(i):
        at = place(layers[i], core, x_chip)
        wait(at, MOST, x_s.at[i], x_r.at[i], to_x)
        send(at, half, dy_s.at[i], dy_r.at[i], to_y)
        send(at, MOST, c_s.at[4 + i], c_r.at[4 + i], to_c)
        at = place(layers[i], core, y_chip)
        wait(at, MOST, y_s.at[i], y_r.at[i], to_y)
        send(at + half, half, dx_s.at[i], dx_r.at[i], to_x)
        send(at, MOST, c_s.at[8 + i], c_r.at[8 + i], to_c)

    def finish(i):
        at = place(layers[i], core, d_chip)
        wait(at, half, dy_s.at[i], dy_r.at[i], to_y)
        wait(at + half, half, dx_s.at[i], dx_r.at[i], to_x)
        send(at, MOST, c_s.at[12 + i], c_r.at[12 + i], to_c)

    def across(i):
        for kind, chip_ in enumerate((chip, x_chip, y_chip, d_chip)):
            at = place(layers[i], 1 - core, chip_)
            wait(at, MOST, c_s.at[4 * kind + i], c_r.at[4 * kind + i], to_c)

    def squares(block):
        wide = block.astype(F32)
        total = wide[:, 0:LANES] * wide[:, 0:LANES]
        for k in range(1, width // LANES):
            piece = wide[:, k * LANES:(k + 1) * LANES]
            total += piece * piece
        return jnp.sum(total.T, axis=0, keepdims=True)

    def norms(first, last):
        @pl.loop(first, last)
        def _(b):
            block = pool[pl.ds(pl.multiple_of(b * LANES, LANES), LANES), :]
            row_norm[pl.ds(b, 1), :] = squares(block)

    step = 512
    steps = rows // step

    def fold(i):
        base = pl.multiple_of(layers[i] * 256, 256)
        for k in range(2):
            block = union[pl.ds(base + k * LANES, LANES), :]
            half_norm[0:1, k * LANES:(k + 1) * LANES] = 0.5 * squares(block)
        shift = half_norm[0:1, :]

        @pl.loop(0, steps)
        def _(b):
            at = pl.ds(pl.multiple_of(b * step, step), step)
            inner = lax.dot_general(
                pool[at, :], union[pl.ds(base, 256), :], NT, preferred_element_type=F32
            )
            gap = shift - inner
            gap = jnp.minimum(gap[:, :LANES], gap[:, LANES:])
            low[at, :] = gap if i == 0 else jnp.minimum(low[at, :], gap)

    pl.semaphore_wait(barrier, len(peers))
    blocks = rows // LANES
    spread(0)
    for k in range(1, 4):
        along_z(k)
    norms(0, blocks // 2)
    relay(0)
    from_z(1)
    norms(blocks // 2, blocks)
    finish(0)
    relay(1)
    from_z(2)
    across(0)
    fold(0)
    finish(1)
    relay(2)
    from_z(3)
    across(1)
    fold(1)
    finish(2)
    relay(3)
    across(2)
    fold(2)
    finish(3)
    across(3)
    fold(3)

    @pl.loop(0, blocks)
    def _(b):
        least = low[pl.ds(pl.multiple_of(b * LANES, LANES), LANES), :].T
        least = jnp.min(least, axis=0, keepdims=True)
        at = pl.ds(b, 1)
        distance = jnp.maximum(row_norm[at, :] + 2.0 * least, 0.0)
        out_ref[at, :] = jnp.minimum(nearest_ref[at, :], distance)

    for c in sent:
        c.wait_send()


def fused(pool, nearest, center_owner, center_offset):
    rows, width = pool.shape
    blocks = rows // LANES
    dma = pltpu.SemaphoreType.DMA
    vmem = pl.BlockSpec(memory_space=pltpu.VMEM)
    result = pl.pallas_call(
        fused_kernel,
        out_shape=jax.ShapeDtypeStruct((blocks, LANES), F32),
        in_specs=[vmem, vmem, vmem, pl.BlockSpec(memory_space=pltpu.HBM)],
        out_specs=vmem,
        scratch_shapes=[
            pltpu.VMEM((rows, width), jnp.bfloat16),
            pltpu.VMEM((1024, width), jnp.bfloat16),
            pltpu.VMEM((MOST, width), F32),
            pltpu.VMEM((blocks, LANES), F32),
            pltpu.VMEM((8, 256), F32),
            pltpu.VMEM((rows, LANES), F32),
            dma((rows // 256,)),
            dma((3,)), dma((3,)),
            dma((4,)), dma((4,)),
            dma((4,)), dma((4,)),
            dma((4,)), dma((4,)),
            dma((4,)), dma((4,)),
            dma((16,)), dma((16,)),
        ],
        compiler_params=pltpu.CompilerParams(
            collective_id=0, has_side_effects=True, vmem_limit_bytes=48 * 1024 * 1024
        ),
    )(center_owner, center_offset, nearest.reshape(blocks, LANES), pool)
    return result.reshape(rows)


def nearest_fold(pool_rows, row_norm, running, fragment):
    center_norm = jnp.einsum("cd,cd->c", fragment, fragment, preferred_element_type=F32)
    total_rows = pool_rows.shape[0]
    block = math.gcd(total_rows, 512)
    blocks = total_rows // block

    def one_block(args):
        block_rows, block_norm, block_near = args
        inner = lax.dot_general(block_rows, fragment, NT, preferred_element_type=F32)
        distance = jnp.maximum(block_norm[:, None] + center_norm[None, :] - 2.0 * inner, 0.0)
        return jnp.minimum(block_near, jnp.min(distance, axis=1))

    result = lax.map(
        one_block,
        (
            pool_rows.reshape(blocks, block, pool_rows.shape[1]),
            row_norm.reshape(blocks, block),
            running.reshape(blocks, block),
        ),
    )
    return result.reshape(total_rows)


def general(pool, nearest, center_owner, center_offset):
    owners = center_owner[0]
    offsets = center_offset[0]
    count = owners.shape[0]
    my_index = lax.axis_index("dev")
    per_device = count // lax.axis_size("dev")
    place = jnp.arange(count, dtype=jnp.int32)
    earlier = (owners[:, None] == owners[None, :]) & (place[None, :] < place[:, None])
    slot_rank = jnp.sum(earlier.astype(jnp.int32), axis=1)
    chosen = (
        (owners == my_index)[None, :]
        & (slot_rank[None, :] == jnp.arange(MOST, dtype=jnp.int32)[:, None])
    ).astype(jnp.int32)
    slot_offsets = jnp.sum(chosen * offsets[None, :], axis=1)
    slot_rows = jnp.take(pool, slot_offsets, axis=0)
    every_slot = lax.all_gather(slot_rows, "dev", axis=0, tiled=True)
    slot_index = owners * MOST + slot_rank
    mine = lax.dynamic_slice_in_dim(slot_index, my_index * per_device, per_device)
    local_centers = jnp.take(every_slot, mine, axis=0)
    row_norm = jnp.einsum("rd,rd->r", pool, pool, preferred_element_type=F32)
    return nearest_fold(
        pool, row_norm, nearest, lax.all_gather(local_centers, ("grp", "dev"), axis=0, tiled=True)
    )


def shards(pool, nearest, center_owner, center_offset):
    groups, devices = lax.axis_size("grp"), lax.axis_size("dev")
    full = center_owner.shape[1] == devices * MOST
    if groups == 4 and devices == 8 and full and pool.shape[0] % 512 == 0:
        return fused(pool, nearest, center_owner, center_offset)
    return general(pool, nearest, center_owner, center_offset)


def solution(mesh):
    in_specs = (P(("grp", "dev"), None), P(("grp", "dev")), P("grp", None), P("grp", None))
    out_specs = P(("grp", "dev"))
    return jax.shard_map(shards, mesh=mesh, in_specs=in_specs, out_specs=out_specs, check_vma=False)
```

time: 112 us -> 35.5 us (0.32)
  waiting for transfers between devices: 52.7 us -> 0 us
  Pallas kernels: 0 us -> 32.5 us
  matrix products: 16.1 us -> 0 us
  between operations: 13.5 us -> 0.01 us
  other arithmetic: 11.5 us -> 0 us
  blocking collectives: 11.3 us -> 0 us
  local copies, waits for them, and re-layouts: 6.15 us -> 2.67 us
    all_gather x1 -> x0, waiting for transfers between devices: 52.7 us -> none  [shards(): lax.all_gather(local_centers, ('grp', 'dev'), axis=0, tiled=True)]
    pallas_call x0 -> x1, Pallas kernels: none -> 32.5 us  [fused(): pl.pallas_call(fused_kernel, out_shape=jax.ShapeDtypeStruct((blocks, LANE...]
    dot_general x6 -> x0, matrix products: 16.1 us -> none  [one_block(): lax.dot_general(block_rows, fragment, (((1,), (1,)), ((), ())), preferred...]
    all_gather x1 -> x0, blocking collectives: 11.3 us -> none  [shards(): every_slot = lax.all_gather(slot_rows, 'dev', axis=0, tiled=True)]
    dot_general x2 -> x0, other arithmetic: 6.3 us -> none  [the longest x1 4.09 us: shards(): jnp.einsum('rd,rd->r', pool, pool, preferred_element_type=jnp.float32)]
    gather x2 -> x0, local copies, waits for them, and re-layouts: 4.9 us -> none  [the longest x1 4.27 us: shards(): slot_rows = jnp.take(pool, slot_offsets, axis=0)]
    unnamed x4 -> x7, local copies, waits for them, and re-layouts: 0.01 us -> 2.67 us
    reduce_sum x2 -> x0, other arithmetic: 1.57 us -> none  [the longest x1 0.79 us: shards(): slot_offsets = jnp.sum(chosen * offsets[None, :], axis=1)]
  transfers between devices with their start and end apart: 1 -> 0, of which waited for: 1 -> 0; matrix products, arithmetic and copies ran while one was open for 4% -> 0% of each run, Pallas kernels for 0% -> 0%
where the time goes in v1:
time: 35.5 us; the launch traced here: 35.2 us
  Pallas kernels  32.5 us (92%)
  local copies, waits for them, and re-layouts  2.67 us (8%)
    pallas_call x1, Pallas kernels, fused(): pl.pallas_call(fused_kernel, out_shape=jax.ShapeDtypeStruct((blocks, LANE...  32.5 us
    unnamed x7, local copies, waits for them, and re-layouts  2.67 us

profile of v1, /device:TPU:0, one launch (start us, length us, event | category | flops | bytes accessed | tf_op | source)
XLA Modules:
  0.0 35.2 jit_solution(10046368561772868462)
XLA Ops:
  0.0 0.0 copy-start
  0.0 0.7 %copy-done = f32[3072]{0:T(1024)S(1)} copy-done((f32[3072]{0:T(1024)S(1)}, f32[3072]{0:T(1024)}, u32[]{:S(2)}) %copy-start) | copy-done | bytes 12312
  0.7 0.0 copy-start.1
  0.7 0.7 %copy-done.1 = s32[1,256]{1,0:T(1,128)S(1)} copy-done((s32[1,256]{1,0:T(1,128)S(1)}, s32[1,256]{1,0:T(1,128)}, u32[]{:S(2)}) %copy-start.1) | copy-done | bytes 1048
  1.4 0.0 copy-start.2
  1.4 0.7 %copy-done.2 = s32[1,256]{1,0:T(1,128)S(1)} copy-done((s32[1,256]{1,0:T(1,128)S(1)}, s32[1,256]{1,0:T(1,128)}, u32[]{:S(2)}) %copy-start.2) | copy-done | bytes 1048
  2.1 32.5 %shard_map.46 = f32[24,128]{1,0:T(8,128)S(1)} custom-call(s32[1,256]{1,0:T(1,128)S(1)} %copy-done.1, s32[1,256]{1,0:T(1,128)S(1)} %copy-done.2, f32[24,128]{1,0:T(8,128)S(1)} %bitcast.3, bf16[3072,1024]{1,0:T(8,128)(2,1)} %pool_hbm.1), custom_call_target="tpu_custom_call" | custom-call | tf_op jit(solution)/shard_map/pallas_call | solution.py:216
  34.6 0.6 %copy.6 = f32[3072]{0:T(1024)} copy(f32[3072]{0:T(1024)S(1)} %bitcast.2) | data formatting | bytes 24576
Async XLA Ops:
  0.0 0.7 %copy-start = (f32[3072]{0:T(1024)S(1)}, f32[3072]{0:T(1024)}, u32[]{:S(2)}) copy-start(f32[3072]{0:T(1024)} %param.5) | copy-start | bytes 36868
  0.7 0.7 %copy-start.1 = (s32[1,256]{1,0:T(1,128)S(1)}, s32[1,256]{1,0:T(1,128)}, u32[]{:S(2)}) copy-start(s32[1,256]{1,0:T(1,128)} %owner_ref.1) | copy-start | bytes 3076
  1.4 0.7 %copy-start.2 = (s32[1,256]{1,0:T(1,128)S(1)}, s32[1,256]{1,0:T(1,128)}, u32[]{:S(2)}) copy-start(s32[1,256]{1,0:T(1,128)} %offset_ref.1) | copy-start | bytes 3076

commit v2 on v1

--- a/solution.py
+++ b/solution.py
@@ -16,14 +16,14 @@
 
 
 def fused_kernel(
-    owner_ref, offset_ref, nearest_ref, pool_hbm, out_ref,
-    pool, union, picked, row_norm, half_norm, low,
-    pool_sem, z_s, z_r, x_s, x_r, y_s, y_r, dx_s, dx_r, dy_s, dy_r, c_s, c_r,
+    owner_hbm, offset_hbm, nearest_hbm, pool_hbm, out_ref,
+    owner_ref, offset_ref, nearest_ref, picked,
+    pool, union, row_norm, half_norm, low,
+    in_sem, pool_sem, z_s, z_r, x_s, x_r, y_s, y_r, g_s, g_r, c_s, c_r,
 ):
     rows, width = pool.shape
     chunk = 256
     chunks = rows // chunk
-    half = MOST // 2
 
     z = lax.axis_index("grp")
     dev = lax.axis_index("dev")
@@ -37,10 +37,11 @@
     x_chip = y * 2 + (1 - x)
     y_chip = (1 - y) * 2 + x
     d_chip = (1 - y) * 2 + (1 - x)
+    g_dev = ((1 - y) * 2 + (1 - x)) * 2 + core
     layers = [z, z + 1 - 2 * (z % 2), (z + 2) % 4, 3 - z]
 
     barrier = pltpu.get_barrier_semaphore()
-    peers = [(z, x_dev), (z, y_dev), (z, c_dev)] + [(l, dev) for l in layers[1:]]
+    peers = [(z, x_dev), (z, y_dev), (z, g_dev), (z, c_dev)] + [(l, dev) for l in layers[1:]]
     for peer in peers:
         pl.semaphore_signal(barrier, inc=1, device_id=peer, device_id_type=MESH)
 
@@ -50,8 +51,15 @@
         )
         for c in range(chunks)
     ]
-    for load in loads:
+    small = [
+        pltpu.make_async_copy(owner_hbm, owner_ref, in_sem.at[0]),
+        pltpu.make_async_copy(offset_hbm, offset_ref, in_sem.at[1]),
+        pltpu.make_async_copy(nearest_hbm, nearest_ref, in_sem.at[2]),
+    ]
+    for load in small + loads:
         load.start()
+    small[0].wait()
+    small[1].wait()
 
     count = owner_ref.shape[1]
     hot = owner_ref[...] == dev
@@ -99,12 +107,13 @@
     def wait(start, size, send_sem, recv_sem, to):
         copy(start, size, send_sem, recv_sem, to).wait_recv()
 
-    to_x, to_y, to_c = (z, x_dev), (z, y_dev), (z, c_dev)
+    to_x, to_y, to_g, to_c = (z, x_dev), (z, y_dev), (z, g_dev), (z, c_dev)
 
     def spread(i):
         at = place(layers[i], core, chip)
         send(at, MOST, x_s.at[i], x_r.at[i], to_x)
         send(at, MOST, y_s.at[i], y_r.at[i], to_y)
+        send(at, MOST, g_s.at[i], g_r.at[i], to_g)
         send(at, MOST, c_s.at[i], c_r.at[i], to_c)
 
     def along_z(k):
@@ -114,20 +123,15 @@
         wait(place(layers[k], core, chip), MOST, z_s.at[k - 1], z_r.at[k - 1], (layers[k], dev))
         spread(k)
 
-    def relay(i):
+    def gather(i):
         at = place(layers[i], core, x_chip)
         wait(at, MOST, x_s.at[i], x_r.at[i], to_x)
-        send(at, half, dy_s.at[i], dy_r.at[i], to_y)
         send(at, MOST, c_s.at[4 + i], c_r.at[4 + i], to_c)
         at = place(layers[i], core, y_chip)
         wait(at, MOST, y_s.at[i], y_r.at[i], to_y)
-        send(at + half, half, dx_s.at[i], dx_r.at[i], to_x)
         send(at, MOST, c_s.at[8 + i], c_r.at[8 + i], to_c)
-
-    def finish(i):
         at = place(layers[i], core, d_chip)
-        wait(at, half, dy_s.at[i], dy_r.at[i], to_y)
-        wait(at + half, half, dx_s.at[i], dx_r.at[i], to_x)
+        wait(at, MOST, g_s.at[i], g_r.at[i], to_g)
         send(at, MOST, c_s.at[12 + i], c_r.at[12 + i], to_c)
 
     def across(i):
@@ -144,22 +148,25 @@
         return jnp.sum(total.T, axis=0, keepdims=True)
 
     def norms(first, last):
-        @pl.loop(first, last)
+        @pl.loop(first, last, unroll=4)
         def _(b):
             block = pool[pl.ds(pl.multiple_of(b * LANES, LANES), LANES), :]
             row_norm[pl.ds(b, 1), :] = squares(block)
 
-    step = 512
+    step = 1536
     steps = rows // step
 
-    def fold(i):
+    def center_norms(i):
         base = pl.multiple_of(layers[i] * 256, 256)
         for k in range(2):
             block = union[pl.ds(base + k * LANES, LANES), :]
             half_norm[0:1, k * LANES:(k + 1) * LANES] = 0.5 * squares(block)
+
+    def fold(i, first, last):
+        base = pl.multiple_of(layers[i] * 256, 256)
         shift = half_norm[0:1, :]
 
-        @pl.loop(0, steps)
+        @pl.loop(first, last)
         def _(b):
             at = pl.ds(pl.multiple_of(b * step, step), step)
             inner = lax.dot_general(
@@ -171,32 +178,34 @@
 
     pl.semaphore_wait(barrier, len(peers))
     blocks = rows // LANES
-    spread(0)
     for k in range(1, 4):
         along_z(k)
-    norms(0, blocks // 2)
-    relay(0)
+    spread(0)
+    norms(0, blocks)
+    small[2].wait()
     from_z(1)
-    norms(blocks // 2, blocks)
-    finish(0)
-    relay(1)
+    gather(0)
     from_z(2)
     across(0)
-    fold(0)
-    finish(1)
-    relay(2)
+    center_norms(0)
+    fold(0, 0, steps // 2)
     from_z(3)
+    fold(0, steps // 2, steps)
+    gather(1)
     across(1)
-    fold(1)
-    finish(2)
-    relay(3)
+    center_norms(1)
+    fold(1, 0, steps // 2)
+    gather(2)
+    fold(1, steps // 2, steps)
+    gather(3)
     across(2)
-    fold(2)
-    finish(3)
+    center_norms(2)
+    fold(2, 0, steps)
     across(3)
-    fold(3)
-
-    @pl.loop(0, blocks)
+    center_norms(3)
+    fold(3, 0, steps)
+
+    @pl.loop(0, blocks, unroll=8)
     def _(b):
         least = low[pl.ds(pl.multiple_of(b * LANES, LANES), LANES), :].T
         least = jnp.min(least, axis=0, keepdims=True)
@@ -213,21 +222,25 @@
     blocks = rows // LANES
     dma = pltpu.SemaphoreType.DMA
     vmem = pl.BlockSpec(memory_space=pltpu.VMEM)
+    hbm = pl.BlockSpec(memory_space=pltpu.HBM)
     result = pl.pallas_call(
         fused_kernel,
         out_shape=jax.ShapeDtypeStruct((blocks, LANES), F32),
-        in_specs=[vmem, vmem, vmem, pl.BlockSpec(memory_space=pltpu.HBM)],
+        in_specs=[hbm, hbm, hbm, hbm],
         out_specs=vmem,
         scratch_shapes=[
+            pltpu.VMEM(center_owner.shape, jnp.int32),
+            pltpu.VMEM(center_offset.shape, jnp.int32),
+            pltpu.VMEM((blocks, LANES), F32),
+            pltpu.VMEM((MOST, width), F32),
             pltpu.VMEM((rows, width), jnp.bfloat16),
             pltpu.VMEM((1024, width), jnp.bfloat16),
-            pltpu.VMEM((MOST, width), F32),
             pltpu.VMEM((blocks, LANES), F32),
             pltpu.VMEM((8, 256), F32),
             pltpu.VMEM((rows, LANES), F32),
+            dma((3,)),
             dma((rows // 256,)),
             dma((3,)), dma((3,)),
-            dma((4,)), dma((4,)),
             dma((4,)), dma((4,)),
             dma((4,)), dma((4,)),
             dma((4,)), dma((4,)),
@@ -291,7 +304,7 @@
 def shards(pool, nearest, center_owner, center_offset):
     groups, devices = lax.axis_size("grp"), lax.axis_size("dev")
     full = center_owner.shape[1] == devices * MOST
-    if groups == 4 and devices == 8 and full and pool.shape[0] % 512 == 0:
+    if groups == 4 and devices == 8 and full and pool.shape[0] % 3072 == 0:
         return fused(pool, nearest, center_owner, center_offset)
     return general(pool, nearest, center_owner, center_offset)
 

time: 35.5 us -> 29.1 us (0.82)
  Pallas kernels: 32.5 us -> 26.2 us
    pallas_call x1, Pallas kernels: 32.5 us -> 26.2 us  [fused(): pl.pallas_call(fused_kernel, out_shape=jax.ShapeDtypeStruct((blocks, LANE...]
where the time goes in v2:
time: 29.1 us; the launch traced here: 28.8 us
  Pallas kernels  26.2 us (90%)
  local copies, waits for them, and re-layouts  2.67 us (9%)
    pallas_call x1, Pallas kernels, fused(): pl.pallas_call(fused_kernel, out_shape=jax.ShapeDtypeStruct((blocks, LANE...  26.2 us
    unnamed x7, local copies, waits for them, and re-layouts  2.67 us

profile of v2, /device:TPU:0, one launch (start us, length us, event | category | flops | bytes accessed | tf_op | source)
XLA Modules:
  0.0 28.8 jit_solution(12956435496548365237)
XLA Ops:
  0.0 0.0 copy-start
  0.0 0.7 %copy-done = f32[3072]{0:T(1024)S(1)} copy-done((f32[3072]{0:T(1024)S(1)}, f32[3072]{0:T(1024)}, u32[]{:S(2)}) %copy-start) | copy-done | bytes 12312
  0.7 0.0 copy-start.1
  0.7 0.7 %copy-done.1 = s32[1,256]{1,0:T(1,128)S(1)} copy-done((s32[1,256]{1,0:T(1,128)S(1)}, s32[1,256]{1,0:T(1,128)}, u32[]{:S(2)}) %copy-start.1) | copy-done | bytes 1048
  1.4 0.0 copy-start.2
  1.4 0.7 %copy-done.2 = s32[1,256]{1,0:T(1,128)S(1)} copy-done((s32[1,256]{1,0:T(1,128)S(1)}, s32[1,256]{1,0:T(1,128)}, u32[]{:S(2)}) %copy-start.2) | copy-done | bytes 1048
  2.1 26.2 %shard_map.46 = f32[24,128]{1,0:T(8,128)S(1)} custom-call(s32[1,256]{1,0:T(1,128)S(1)} %copy-done.1, s32[1,256]{1,0:T(1,128)S(1)} %copy-done.2, f32[24,128]{1,0:T(8,128)S(1)} %bitcast.3, bf16[3072,1024]{1,0:T(8,128)(2,1)} %pool_hbm.1), custom_call_target="tpu_custom_call" | custom-call | tf_op jit(solution)/shard_map/pallas_call | solution.py:226
  28.2 0.6 %copy.6 = f32[3072]{0:T(1024)} copy(f32[3072]{0:T(1024)S(1)} %bitcast.2) | data formatting | bytes 24576
Async XLA Ops:
  0.0 0.7 %copy-start = (f32[3072]{0:T(1024)S(1)}, f32[3072]{0:T(1024)}, u32[]{:S(2)}) copy-start(f32[3072]{0:T(1024)} %param.5) | copy-start | bytes 36868
  0.7 0.7 %copy-start.1 = (s32[1,256]{1,0:T(1,128)S(1)}, s32[1,256]{1,0:T(1,128)}, u32[]{:S(2)}) copy-start(s32[1,256]{1,0:T(1,128)} %owner_hbm.1) | copy-start | bytes 3076
  1.4 0.7 %copy-start.2 = (s32[1,256]{1,0:T(1,128)S(1)}, s32[1,256]{1,0:T(1,128)}, u32[]{:S(2)}) copy-start(s32[1,256]{1,0:T(1,128)} %offset_hbm.1) | copy-start | bytes 3076
